TPU v7x, 32 devices: a whole 2x2x4 slice. The times are simulated.
32 devices in a mesh: segment: 2 (over x), tensor: 16 (over z, y, core).
Axes of the slice: x: 2, y: 2, z: 4, core: 2. Of those that a mesh axis runs over, the one named last changes fastest.
Arguments:
- step_inputs: bfloat16 [3, 16, 8192], P(None, None, 'tensor'), may hold values from -6 to 6
- norm_gain: float32 [2, 8192], P('segment'), may hold values from 0.1 to 1.9
- query_weight: bfloat16 [2, 8192, 8192], P('segment', None, 'tensor'), may hold values from -0.0625 to 0.0625
- kv_weight: bfloat16 [2, 8192, 2, 1024], P('segment', None, None, 'tensor'), may hold values from -0.125 to 0.125
- out_weight: bfloat16 [2, 8192, 8192], P('segment', None, 'tensor'), may hold values from -0.125 to 0.125
- kv_cache: bfloat16 [2, 16, 3, 128, 256], P('segment', 'tensor'), as said below
- block_table: int32 [16, 2], replicated, may hold values from 0 to 2, as said below
- prefix_len: int32 [16], replicated, may hold values from 1 to 256, as said below
- parents: int32 [3, 16], replicated, may hold values from 0 to 15
Outputs:
- received: bfloat16 [2, 3, 16, 8192], P('segment', None, None, 'tensor')
Inputs may be any that keep to these rules, and one draw needn't show every extreme that they name: `block_table`: every row of one source has the same first entry; its second entry is one of two blocks of that source, each of them used by some row; no block serves two sources. `prefix_len`: some row holds 256 tokens. `kv_cache`: copies c and c' are equal when c * 64 // (number of copies) // 8 equals the same for c'.
All inputs are finite; a program needn't handle non-finite values.
Results may differ from a plain program's by a relative error of at most 0.012.
The roundings to bfloat16 on the way count: a program that leaves them out, or rounds other values in their place, can miss the bound.
Values may be sent and summed in bfloat16 or wider, within the bound.
A program may use at most 64 MiB of HBM per device.

v0:
```python
import jax
import jax.numpy as jnp
from jax import lax
from jax.sharding import PartitionSpec as P

KV_HEADS = 8
HEAD_SIZE = 128
BEAMS = 16
BLOCK = 128
STEPS = 3
SOURCES = 1
GROUP = 8
ROPE_BASE = 1000000.0
NORM_EPS = 1e-06
MASK_FLOOR = -1e30


def shifted(block, axis, distance):
    devices = range(lax.axis_size(axis))
    route = [((i - distance) % len(devices), i) for i in devices]
    return lax.ppermute(block, axis, route)


def normalize(rows_in, gain):
    widened = rows_in.astype(jnp.float32)
    mean_square = jnp.mean(widened * widened, axis=-1, keepdims=True)
    return (widened * lax.rsqrt(mean_square + NORM_EPS) * gain).astype(jnp.bfloat16)


def rotate(values, positions):
    half_size = values.shape[-1] // 2
    exponent = jnp.arange(half_size, dtype=jnp.float32) * (2.0 / values.shape[-1])
    frequency = jnp.power(jnp.float32(ROPE_BASE), -exponent)
    angles = positions.astype(jnp.float32)[:, None] * frequency[None, :]
    angles = jnp.concatenate([angles, angles], axis=-1)[:, None, :]
    front_part = values[..., :half_size]
    back_part = values[..., half_size:]
    turned = jnp.concatenate([-back_part, front_part], axis=-1)
    return values * jnp.cos(angles) + turned * jnp.sin(angles)


def ancestry(parents):
    rows_all = parents.shape[1]
    source_start = jnp.arange(rows_all, dtype=jnp.int32) // BEAMS * BEAMS
    lineage = []
    root_table = []
    for later_step in range(STEPS):
        current = jnp.arange(rows_all, dtype=jnp.int32)
        lineage_list = [current]
        for earlier in range(later_step, 0, -1):
            current = source_start + parents[earlier][current]
            lineage_list.append(current)
        lineage_list = lineage_list[::-1] + [current] * (STEPS - later_step - 1)
        lineage.append(jnp.stack(lineage_list))
        root_table.append(source_start + parents[0][current])
    return (jnp.stack(lineage), jnp.stack(root_table))


def per_device(
    step_inputs,
    norm_gain,
    query_weight,
    kv_weight,
    out_weight,
    kv_cache,
    block_table,
    prefix_len,
    parents,
):
    segments = lax.axis_size("segment")
    segment_id = lax.axis_index("segment")
    device_id = lax.axis_index("tensor")
    local_width = step_inputs.shape[2]
    rows_all = step_inputs.shape[1]
    head_count = query_weight.shape[2] // HEAD_SIZE
    kv_owner = device_id * head_count // GROUP
    score_scale = HEAD_SIZE ** (-0.5)
    lineage, root_table = ancestry(parents)
    gain = norm_gain[0]
    query_local = query_weight[0]
    kv_local = kv_weight[0]
    out_local = out_weight[0]
    cache_local = kv_cache[0, 0]

    def project_rows(piece):
        return jnp.dot(piece, out_local, preferred_element_type=jnp.float32)

    def advance(loop_state, tick_index, item_base, item_count):
        incoming, history, received = loop_state
        local_item = tick_index - segment_id
        active = (local_item >= 0) & (local_item < item_count)
        item_index = item_base + jnp.clip(local_item, 0, item_count - 1)
        step_index = item_index // SOURCES
        source = item_index % SOURCES
        row_start = source * BEAMS
        fresh_rows = lax.dynamic_slice(
            step_inputs, (step_index, row_start, 0), (1, BEAMS, local_width)
        )[0]
        current = jnp.where(segment_id == 0, fresh_rows, incoming)
        full_rows = lax.all_gather(current, "tensor", axis=1, tiled=True)
        normed = normalize(full_rows, gain)
        queries = jnp.dot(normed, query_local, preferred_element_type=jnp.float32).reshape(
            BEAMS, head_count, HEAD_SIZE
        )
        partial_kv = jnp.einsum(
            "rd,dkc->rkc", normed, kv_local, preferred_element_type=jnp.float32
        ).astype(jnp.bfloat16)
        gathered_kv = lax.all_gather(partial_kv, "tensor", axis=2, tiled=True)
        gathered_kv = gathered_kv.reshape(BEAMS, 2, HEAD_SIZE, KV_HEADS)
        own_kv = lax.dynamic_slice_in_dim(gathered_kv, kv_owner, 1, 3)[..., 0]
        lineage_rows = lax.dynamic_slice(lineage, (step_index, 0, row_start), (1, STEPS, BEAMS))[0]
        root_rows = lax.dynamic_slice(root_table, (step_index, row_start), (1, BEAMS))[0]
        lengths = prefix_len[root_rows]
        positions = lengths + step_index
        new_key = rotate(own_kv[:, 0:1].astype(jnp.float32), positions).astype(jnp.bfloat16)[:, 0]
        turned_query = rotate(queries, positions).astype(jnp.bfloat16)
        new_entry = jnp.stack([new_key, own_kv[:, 1]], axis=1)
        updated = lax.dynamic_update_slice(history, new_entry[None], (step_index, row_start, 0, 0))
        history = jnp.where(active, updated, history)
        past = history[jnp.arange(STEPS, dtype=jnp.int32)[:, None], lineage_rows]
        history_mask = jnp.arange(STEPS, dtype=jnp.int32) <= step_index
        prefix_mask = jnp.arange(2 * BLOCK, dtype=jnp.int32)[None, :] < lengths[:, None]
        table_rows = block_table[root_rows]
        blocks = cache_local[table_rows].reshape(BEAMS, 2 * BLOCK, 2 * HEAD_SIZE)
        prefix_scores = jnp.einsum(
            "rhd,rkd->rhk",
            turned_query,
            blocks[:, :, :HEAD_SIZE],
            preferred_element_type=jnp.float32,
        )
        prefix_scores = jnp.where(prefix_mask[:, None, :], prefix_scores * score_scale, MASK_FLOOR)
        history_scores = (
            jnp.einsum(
                "rhd,trd->rht", turned_query, past[:, :, 0], preferred_element_type=jnp.float32
            )
            * score_scale
        )
        history_scores = jnp.where(history_mask[None, None, :], history_scores, MASK_FLOOR)
        highest = jnp.maximum(jnp.max(prefix_scores, axis=-1), jnp.max(history_scores, axis=-1))[
            ..., None
        ]
        prefix_exp = jnp.exp(prefix_scores - highest)
        history_exp = jnp.exp(history_scores - highest)
        denominator = jnp.sum(prefix_exp, axis=-1, keepdims=True) + jnp.sum(
            history_exp, axis=-1, keepdims=True
        )
        prefix_probs = (prefix_exp / denominator).astype(jnp.bfloat16)
        history_probs = (history_exp / denominator).astype(jnp.bfloat16)
        mixture = jnp.einsum(
            "rhk,rkd->rhd",
            prefix_probs,
            blocks[:, :, HEAD_SIZE:],
            preferred_element_type=jnp.float32,
        )
        mixture = mixture + jnp.einsum(
            "rht,trd->rhd", history_probs, past[:, :, 1], preferred_element_type=jnp.float32
        )
        attended = mixture.reshape(BEAMS, head_count * HEAD_SIZE).astype(jnp.bfloat16)
        update = project_rows(lax.all_gather(attended, "tensor", axis=1, tiled=True))
        result = (current.astype(jnp.float32) + update).astype(jnp.bfloat16)
        passed = shifted(result, "segment", 1)
        sender = (segment_id + segments - 1) % segments
        sent_local = tick_index - sender
        sent_valid = (sent_local >= 0) & (sent_local < item_count)
        sent_item = item_base + jnp.clip(sent_local, 0, item_count - 1)
        sent_step = sent_item // SOURCES
        sent_row = sent_item % SOURCES * BEAMS
        stored = lax.dynamic_update_slice(received, passed[None], (sent_step, sent_row, 0))
        received = jnp.where(sent_valid, stored, received)
        return (passed, history, received)

    loop_state = (
        jnp.zeros((BEAMS, local_width), jnp.bfloat16),
        jnp.zeros((STEPS, rows_all, 2, HEAD_SIZE), jnp.bfloat16),
        jnp.zeros((STEPS, rows_all, local_width), jnp.bfloat16),
    )
    sweep_loop_state = loop_state
    item_count = STEPS * SOURCES

    def scan_step(state_in, tick_index):
        return (advance(state_in, tick_index, 0, item_count), None)

    ticks = jnp.arange(item_count + segments - 1, dtype=jnp.int32)
    sweep_loop_state, unused = lax.scan(scan_step, sweep_loop_state, ticks)
    loop_state = sweep_loop_state
    return loop_state[2][None]


def solution(mesh):
    return jax.shard_map(
        per_device,
        mesh=mesh,
        in_specs=(
            P(None, None, "tensor"),
            P("segment", None),
            P("segment", None, "tensor"),
            P("segment", None, None, "tensor"),
            P("segment", None, "tensor"),
            P("segment", "tensor", None, None, None),
            P(),
            P(),
            P(),
        ),
        out_specs=P("segment", None, None, "tensor"),
        check_vma=False,
    )
```

profile of v0, /device:TPU:0, one launch (start us, length us, event | category | flops | bytes accessed | tf_op | source)
XLA Modules:
  0.0 343.2 jit_solution(172588675042118891)
XLA Ops:
  5.4 337.2 %while.17 = (s32[]{:T(128)}, bf16[16,512]{1,0:T(8,128)(2,1)S(1)}, bf16[3,16,2,128]{3,2,1,0:T(2,128)(2,1)S(1)}, bf16[3,16,512]{2,1,0:T(8,128)(2,1)S(1)}, pred[]{:...) while((s32[]{:T(128)}, bf16[16,512]{1,0:T(8,128)(2,1)S(1)}, ...), condition=%wide.region_6.7_spmd, body=%wide.region_0.6_spmd.sunk | while | flops 312203328 | bytes 28216092 | solution.py:184
  8.1 23.8 %all_gather.24 = bf16[16,8192]{1,0:T(8,128)(2,1)S(1)} all-gather(bf16[16,512]{1,0:T(8,128)(2,1)S(1)} %bitcast_select_fusion.3), channel_id=1, replica_groups=mesh['segment'=2,'tensor'=16] {'tensor'}, dimensions={1}, use_global_device_ids=true | all-gather | bytes 278528 | tf_op jit(solution)/shard_map/while/body/eval_jaxpr/all_gather | solution.py:100
  32.1 0.9 convolution_convert_fusion.2
  33.2 18.9 %all_gather.25 = bf16[16,2,1024]{0,1,2:T(2,128)(2,1)S(1)} all-gather(bf16[16,2,64]{0,1,2:T(2,128)(2,1)S(1)} %copy.77), channel_id=1, replica_groups=mesh['segment'=2,'tensor'=16] {'tensor'}, dimensions={2}, use_global_device_ids=true | all-gather | bytes 69632 | tf_op jit(solution)/shard_map/while/body/eval_jaxpr/all_gather | solution.py:108
  53.2 0.9 gather_fusion.3
  54.1 4.6 %fusion.83 = f32[16,512]{1,0:T(8,128)S(1)} fusion(bf16[8192,512]{1,0:T(8,128)(2,1)} %get-tuple-element.631, bf16[16,8192]{1,0:T(8,128)(2,1)S(1)} %all_gather.24, f32[8192]{0:T(1024)S(1)} %bitcast.161, f32[16]{0:T(128)S(1)} %add_rsqrt_fusion.2), kind=kOutput, calls=%fused_computation.31.clone.1 | convolution fusion | flops 134742016 | bytes 8716352 | tf_op jit(solution)/shard_map/while/body/eval_jaxpr/dot_general | solution.py:102
  59.7 2.0 gather_fusion.1
  62.0 1.7 fusion.86
  63.9 1.5 fusion.94
  65.7 19.5 %all_gather.26 = bf16[16,8192]{1,0:T(8,128)(2,1)S(1)} all-gather(bf16[16,512]{1,0:T(8,128)(2,1)S(1)} %bitcast.164), channel_id=1, replica_groups=mesh['segment'=2,'tensor'=16] {'tensor'}, dimensions={1}, use_global_device_ids=true | all-gather | bytes 278528 | tf_op jit(solution)/shard_map/while/body/eval_jaxpr/all_gather | solution.py:159
  85.2 4.6 %fusion.96 = bf16[16,512]{1,0:T(8,128)(2,1)S(1)} fusion(bf16[16,8192]{1,0:T(8,128)(2,1)S(1)} %all_gather.26, bf16[8192,512]{1,0:T(8,128)(2,1)} %get-tuple-element.637, bf16[16,512]{1,0:T(8,128)(2,1)S(1)} %bitcast_select_fusion.3), kind=kOutput, calls=%fused_computation.17.clone.1 | convolution fusion | flops 134242304 | bytes 8683520 | tf_op jit(solution)/shard_map/while/body/eval_jaxpr/dot_general | solution.py:86
  89.8 1.5 collective-permute-start
  91.9 1.6 collective-permute-done
  96.3 18.2 %all_gather.24 = bf16[16,8192]{1,0:T(8,128)(2,1)S(1)} all-gather(bf16[16,512]{1,0:T(8,128)(2,1)S(1)} %bitcast_select_fusion.3), channel_id=1, replica_groups=mesh['segment'=2,'tensor'=16] {'tensor'}, dimensions={1}, use_global_device_ids=true | all-gather | bytes 278528 | tf_op jit(solution)/shard_map/while/body/eval_jaxpr/all_gather | solution.py:100
  114.7 0.9 convolution_convert_fusion.2
  115.8 20.3 %all_gather.25 = bf16[16,2,1024]{0,1,2:T(2,128)(2,1)S(1)} all-gather(bf16[16,2,64]{0,1,2:T(2,128)(2,1)S(1)} %copy.77), channel_id=1, replica_groups=mesh['segment'=2,'tensor'=16] {'tensor'}, dimensions={2}, use_global_device_ids=true | all-gather | bytes 69632 | tf_op jit(solution)/shard_map/while/body/eval_jaxpr/all_gather | solution.py:108
  138.1 4.6 %fusion.83 = f32[16,512]{1,0:T(8,128)S(1)} fusion(bf16[8192,512]{1,0:T(8,128)(2,1)} %get-tuple-element.631, bf16[16,8192]{1,0:T(8,128)(2,1)S(1)} %all_gather.24, f32[8192]{0:T(1024)S(1)} %bitcast.161, f32[16]{0:T(128)S(1)} %add_rsqrt_fusion.2), kind=kOutput, calls=%fused_computation.31.clone.1 | convolution fusion | flops 134742016 | bytes 8716352 | tf_op jit(solution)/shard_map/while/body/eval_jaxpr/dot_general | solution.py:102
  143.7 2.0 gather_fusion.1
  146.0 1.7 fusion.86
  147.9 1.5 fusion.94
  149.7 18.2 %all_gather.26 = bf16[16,8192]{1,0:T(8,128)(2,1)S(1)} all-gather(bf16[16,512]{1,0:T(8,128)(2,1)S(1)} %bitcast.164), channel_id=1, replica_groups=mesh['segment'=2,'tensor'=16] {'tensor'}, dimensions={1}, use_global_device_ids=true | all-gather | bytes 278528 | tf_op jit(solution)/shard_map/while/body/eval_jaxpr/all_gather | solution.py:159
  167.8 4.6 %fusion.96 = bf16[16,512]{1,0:T(8,128)(2,1)S(1)} fusion(bf16[16,8192]{1,0:T(8,128)(2,1)S(1)} %all_gather.26, bf16[8192,512]{1,0:T(8,128)(2,1)} %get-tuple-element.637, bf16[16,512]{1,0:T(8,128)(2,1)S(1)} %bitcast_select_fusion.3), kind=kOutput, calls=%fused_computation.17.clone.1 | convolution fusion | flops 134242304 | bytes 8683520 | tf_op jit(solution)/shard_map/while/body/eval_jaxpr/dot_general | solution.py:86
  172.4 1.5 collective-permute-start
  174.5 1.6 collective-permute-done
  178.9 19.5 %all_gather.24 = bf16[16,8192]{1,0:T(8,128)(2,1)S(1)} all-gather(bf16[16,512]{1,0:T(8,128)(2,1)S(1)} %bitcast_select_fusion.3), channel_id=1, replica_groups=mesh['segment'=2,'tensor'=16] {'tensor'}, dimensions={1}, use_global_device_ids=true | all-gather | bytes 278528 | tf_op jit(solution)/shard_map/while/body/eval_jaxpr/all_gather | solution.py:100
  198.6 0.9 convolution_convert_fusion.2
  199.6 18.9 %all_gather.25 = bf16[16,2,1024]{0,1,2:T(2,128)(2,1)S(1)} all-gather(bf16[16,2,64]{0,1,2:T(2,128)(2,1)S(1)} %copy.77), channel_id=1, replica_groups=mesh['segment'=2,'tensor'=16] {'tensor'}, dimensions={2}, use_global_device_ids=true | all-gather | bytes 69632 | tf_op jit(solution)/shard_map/while/body/eval_jaxpr/all_gather | solution.py:108
  219.7 0.9 gather_fusion.3
  220.6 4.6 %fusion.83 = f32[16,512]{1,0:T(8,128)S(1)} fusion(bf16[8192,512]{1,0:T(8,128)(2,1)} %get-tuple-element.631, bf16[16,8192]{1,0:T(8,128)(2,1)S(1)} %all_gather.24, f32[8192]{0:T(1024)S(1)} %bitcast.161, f32[16]{0:T(128)S(1)} %add_rsqrt_fusion.2), kind=kOutput, calls=%fused_computation.31.clone.1 | convolution fusion | flops 134742016 | bytes 8716352 | tf_op jit(solution)/shard_map/while/body/eval_jaxpr/dot_general | solution.py:102
  226.2 2.0 gather_fusion.1
  228.4 1.7 fusion.86
  230.4 1.5 fusion.94
  232.1 19.5 %all_gather.26 = bf16[16,8192]{1,0:T(8,128)(2,1)S(1)} all-gather(bf16[16,512]{1,0:T(8,128)(2,1)S(1)} %bitcast.164), channel_id=1, replica_groups=mesh['segment'=2,'tensor'=16] {'tensor'}, dimensions={1}, use_global_device_ids=true | all-gather | bytes 278528 | tf_op jit(solution)/shard_map/while/body/eval_jaxpr/all_gather | solution.py:159
  251.6 4.6 %fusion.96 = bf16[16,512]{1,0:T(8,128)(2,1)S(1)} fusion(bf16[16,8192]{1,0:T(8,128)(2,1)S(1)} %all_gather.26, bf16[8192,512]{1,0:T(8,128)(2,1)} %get-tuple-element.637, bf16[16,512]{1,0:T(8,128)(2,1)S(1)} %bitcast_select_fusion.3), kind=kOutput, calls=%fused_computation.17.clone.1 | convolution fusion | flops 134242304 | bytes 8683520 | tf_op jit(solution)/shard_map/while/body/eval_jaxpr/dot_general | solution.py:86
  256.2 1.5 collective-permute-start
  258.3 1.6 collective-permute-done
  262.7 18.2 %all_gather.24 = bf16[16,8192]{1,0:T(8,128)(2,1)S(1)} all-gather(bf16[16,512]{1,0:T(8,128)(2,1)S(1)} %bitcast_select_fusion.3), channel_id=1, replica_groups=mesh['segment'=2,'tensor'=16] {'tensor'}, dimensions={1}, use_global_device_ids=true | all-gather | bytes 278528 | tf_op jit(solution)/shard_map/while/body/eval_jaxpr/all_gather | solution.py:100
  281.1 0.9 convolution_convert_fusion.2
  282.2 20.3 %all_gather.25 = bf16[16,2,1024]{0,1,2:T(2,128)(2,1)S(1)} all-gather(bf16[16,2,64]{0,1,2:T(2,128)(2,1)S(1)} %copy.77), channel_id=1, replica_groups=mesh['segment'=2,'tensor'=16] {'tensor'}, dimensions={2}, use_global_device_ids=true | all-gather | bytes 69632 | tf_op jit(solution)/shard_map/while/body/eval_jaxpr/all_gather | solution.py:108
  303.6 0.9 gather_fusion.3
  304.5 4.6 %fusion.83 = f32[16,512]{1,0:T(8,128)S(1)} fusion(bf16[8192,512]{1,0:T(8,128)(2,1)} %get-tuple-element.631, bf16[16,8192]{1,0:T(8,128)(2,1)S(1)} %all_gather.24, f32[8192]{0:T(1024)S(1)} %bitcast.161, f32[16]{0:T(128)S(1)} %add_rsqrt_fusion.2), kind=kOutput, calls=%fused_computation.31.clone.1 | convolution fusion | flops 134742016 | bytes 8716352 | tf_op jit(solution)/shard_map/while/body/eval_jaxpr/dot_general | solution.py:102
  310.1 2.0 gather_fusion.1
  312.3 1.7 fusion.86
  314.3 1.5 fusion.94
  316.0 18.2 %all_gather.26 = bf16[16,8192]{1,0:T(8,128)(2,1)S(1)} all-gather(bf16[16,512]{1,0:T(8,128)(2,1)S(1)} %bitcast.164), channel_id=1, replica_groups=mesh['segment'=2,'tensor'=16] {'tensor'}, dimensions={1}, use_global_device_ids=true | all-gather | bytes 278528 | tf_op jit(solution)/shard_map/while/body/eval_jaxpr/all_gather | solution.py:159
  334.2 4.6 %fusion.96 = bf16[16,512]{1,0:T(8,128)(2,1)S(1)} fusion(bf16[16,8192]{1,0:T(8,128)(2,1)S(1)} %all_gather.26, bf16[8192,512]{1,0:T(8,128)(2,1)} %get-tuple-element.637, bf16[16,512]{1,0:T(8,128)(2,1)S(1)} %bitcast_select_fusion.3), kind=kOutput, calls=%fused_computation.17.clone.1 | convolution fusion | flops 134242304 | bytes 8683520 | tf_op jit(solution)/shard_map/while/body/eval_jaxpr/dot_general | solution.py:86
  338.8 1.5 collective-permute-start
  340.9 1.6 collective-permute-done
  (221 shorter events, 27.3 us)
Async XLA Ops:
  0.0 5.2 %copy-start.5 = (s32[16,2]{0,1:T(2,128)S(1)}, s32[16,2]{0,1:T(2,128)}, u32[]{:S(2)}) copy-start(s32[16,2]{0,1:T(2,128)} %param.17) | copy-start | bytes 388
  0.0 5.3 %copy-start.1 = (bf16[1,1,3,128,256]{4,3,2,1,0:T(8,128)(2,1)S(1)}, bf16[1,1,3,128,256]{4,3,2,1,0:T(8,128)(2,1)}, u32[]{:S(2)}) copy-start(bf16[1,1,3,128,256]{4,3,2,1,0:T(8,128)(2,1)} %param.16) | copy-start | bytes 589828
  0.0 5.3 %copy-start.2 = (bf16[1,8192,2,64]{1,3,2,0:T(8,128)(2,1)S(1)}, bf16[1,8192,2,64]{1,3,2,0:T(8,128)(2,1)}, u32[]{:S(2)}) copy-start(bf16[1,8192,2,64]{1,3,2,0:T(8,128)(2,1)} %param.14) | copy-start | bytes 6291460
  0.0 5.3 %copy-start.3 = (f32[1,8192]{1,0:T(1,128)S(1)}, f32[1,8192]{1,0:T(1,128)}, u32[]{:S(2)}) copy-start(f32[1,8192]{1,0:T(1,128)} %param.12) | copy-start | bytes 98308
  0.0 5.3 %copy-start = (s32[16]{0:T(128)S(1)}, s32[16]{0:T(128)}, u32[]{:S(2)}) copy-start(s32[16]{0:T(128)} %param.18) | copy-start | bytes 196
  89.8 3.8 %collective-permute-start = (bf16[16,512]{1,0:T(8,128)(2,1)S(1)}, bf16[16,512]{1,0:T(8,128)(2,1)S(1)}, u32[]{:S(2)}, u32[]{:S(2)}) collective-permute-start(bf16[16,512]{1,0:T(8,128)(2,1)S(1)} %fusion.96), channel_id=1, source_target_pairs={{16,0},{0,16},{17,1},{1,17},{18,2},{2,18},{19,3},{3,19},{20,4},{4,... | collective-permute-start | bytes 49160 | tf_op jit(solution)/shard_map/while/body/eval_jaxpr/ppermute | solution.py:21
  172.4 3.8 %collective-permute-start = (bf16[16,512]{1,0:T(8,128)(2,1)S(1)}, bf16[16,512]{1,0:T(8,128)(2,1)S(1)}, u32[]{:S(2)}, u32[]{:S(2)}) collective-permute-start(bf16[16,512]{1,0:T(8,128)(2,1)S(1)} %fusion.96), channel_id=1, source_target_pairs={{16,0},{0,16},{17,1},{1,17},{18,2},{2,18},{19,3},{3,19},{20,4},{4,... | collective-permute-start | bytes 49160 | tf_op jit(solution)/shard_map/while/body/eval_jaxpr/ppermute | solution.py:21
  256.2 3.8 %collective-permute-start = (bf16[16,512]{1,0:T(8,128)(2,1)S(1)}, bf16[16,512]{1,0:T(8,128)(2,1)S(1)}, u32[]{:S(2)}, u32[]{:S(2)}) collective-permute-start(bf16[16,512]{1,0:T(8,128)(2,1)S(1)} %fusion.96), channel_id=1, source_target_pairs={{16,0},{0,16},{17,1},{1,17},{18,2},{2,18},{19,3},{3,19},{20,4},{4,... | collective-permute-start | bytes 49160 | tf_op jit(solution)/shard_map/while/body/eval_jaxpr/ppermute | solution.py:21
  338.8 3.8 %collective-permute-start = (bf16[16,512]{1,0:T(8,128)(2,1)S(1)}, bf16[16,512]{1,0:T(8,128)(2,1)S(1)}, u32[]{:S(2)}, u32[]{:S(2)}) collective-permute-start(bf16[16,512]{1,0:T(8,128)(2,1)S(1)} %fusion.96), channel_id=1, source_target_pairs={{16,0},{0,16},{17,1},{1,17},{18,2},{2,18},{19,3},{3,19},{20,4},{4,... | collective-permute-start | bytes 49160 | tf_op jit(solution)/shard_map/while/body/eval_jaxpr/ppermute | solution.py:21
  342.5 0.6 copy-start.4
where the time goes:
time: 344 us; the launch traced here: 343 us
  blocking collectives  233 us (68%)
  matrix products  54.9 us (16%)
  local copies, waits for them, and re-layouts  27.8 us (8%)
  other arithmetic  8.74 us (3%)
  waiting for transfers between devices  6.44 us (2%)
  starting transfers between devices  6.02 us (2%)
  loops' own time  5.8 us (2%)
    all_gather x4, blocking collectives, advance(): full_rows = lax.all_gather(current, 'tensor', axis=1, tiled=True)  79.6 us
    all_gather x4, blocking collectives, advance(): gathered_kv = lax.all_gather(partial_kv, 'tensor', axis=2, tiled=True)  78.3 us
    all_gather x4, blocking collectives, advance(): lax.all_gather(attended, 'tensor', axis=1, tiled=True)  75.3 us
    dot_general x4, matrix products, advance(): jnp.dot(normed, query_local, preferred_element_type=jnp.float32)  18.5 us
    dot_general x4, matrix products, project_rows(): return jnp.dot(piece, out_local, preferred_element_type=jnp.float32)  18.3 us
    gather x4, local copies, waits for them, and re-layouts, advance(): blocks = cache_local[table_rows].reshape(BEAMS, 2 * BLOCK, 2 * HEAD_SIZE)  8.11 us
  transfers between devices with their start and end apart: 4, of which 4 were waited for; matrix products, arithmetic and copies ran while one was open for 0% of the time, Pallas kernels for 0%

commit v1 on v0

--- a/solution.py
+++ b/solution.py
@@ -105,7 +105,14 @@
         partial_kv = jnp.einsum(
             "rd,dkc->rkc", normed, kv_local, preferred_element_type=jnp.float32
         ).astype(jnp.bfloat16)
-        gathered_kv = lax.all_gather(partial_kv, "tensor", axis=2, tiled=True)
+        ways, here = (lax.axis_size("tensor"), lax.axis_index("tensor"))
+        gathered_kv, reach = (partial_kv, 1)
+        while reach < ways:
+            theirs = lax.ppermute(gathered_kv, "tensor", [(d, d ^ reach) for d in range(ways)])
+            mine_first = jnp.concatenate([gathered_kv, theirs], axis=2)
+            theirs_first = jnp.concatenate([theirs, gathered_kv], axis=2)
+            gathered_kv = jnp.where(here & reach == 0, mine_first, theirs_first)
+            reach = 2 * reach
         gathered_kv = gathered_kv.reshape(BEAMS, 2, HEAD_SIZE, KV_HEADS)
         own_kv = lax.dynamic_slice_in_dim(gathered_kv, kv_owner, 1, 3)[..., 0]
         lineage_rows = lax.dynamic_slice(lineage, (step_index, 0, row_start), (1, STEPS, BEAMS))[0]

time: 344 us -> 318 us (0.924)
  blocking collectives: 233 us -> 155 us
  waiting for transfers between devices: 6.44 us -> 53.1 us
    all_gather x4 -> x0, blocking collectives: 78.3 us -> none  [advance(): gathered_kv = lax.all_gather(partial_kv, 'tensor', axis=2, tiled=True)]
    ppermute x0 -> x16, waiting for transfers between devices: none -> 46.7 us  [advance(): lax.ppermute(gathered_kv, 'tensor', [(d, d ^ reach) for d in range(ways)])]
    all_gather x4, blocking collectives: 75.3 us -> 71.4 us  [advance(): lax.all_gather(attended, 'tensor', axis=1, tiled=True)]
    all_gather x4, blocking collectives: 79.6 us -> 83.5 us  [advance(): full_rows = lax.all_gather(current, 'tensor', axis=1, tiled=True)]
  transfers between devices with their start and end apart: 4 -> 20, of which waited for: 4 -> 16; matrix products, arithmetic and copies ran while one was open for 0% -> 14% of each run, Pallas kernels for 0% -> 0%
where the time goes in v1:
time: 318 us; the launch traced here: 317 us
  blocking collectives  155 us (49%)
  matrix products  54.9 us (17%)
  waiting for transfers between devices  53.1 us (17%)
  local copies, waits for them, and re-layouts  29.1 us (9%)
  other arithmetic  10.9 us (3%)
  starting transfers between devices  7.83 us (2%)
  loops' own time  6.08 us (2%)
    all_gather x4, blocking collectives, advance(): full_rows = lax.all_gather(current, 'tensor', axis=1, tiled=True)  83.5 us
    all_gather x4, blocking collectives, advance(): lax.all_gather(attended, 'tensor', axis=1, tiled=True)  71.4 us
    ppermute x16, waiting for transfers between devices, advance(): lax.ppermute(gathered_kv, 'tensor', [(d, d ^ reach) for d in range(ways)])  46.7 us
    dot_general x4, matrix products, advance(): jnp.dot(normed, query_local, preferred_element_type=jnp.float32)  18.5 us
    dot_general x4, matrix products, project_rows(): return jnp.dot(piece, out_local, preferred_element_type=jnp.float32)  18.3 us
    gather x4, local copies, waits for them, and re-layouts, advance(): blocks = cache_local[table_rows].reshape(BEAMS, 2 * BLOCK, 2 * HEAD_SIZE)  8.03 us
    dot_general x4, matrix products, advance(): jnp.einsum('rhd,rkd->rhk', turned_query, blocks[:, :, :HEAD_SIZE], prefer...  6.74 us
    ppermute x4, waiting for transfers between devices, shifted(): return lax.ppermute(block, axis, route)  6.4 us
  transfers between devices with their start and end apart: 20, of which 16 were waited for; matrix products, arithmetic and copies ran while one was open for 14% of the time, Pallas kernels for 0%

profile of v1, /device:TPU:0, one launch (start us, length us, event | category | flops | bytes accessed | tf_op | source)
XLA Modules:
  0.0 317.1 jit_solution(5508007048366915790)
XLA Ops:
  5.4 311.1 %while.17 = (s32[]{:T(128)}, bf16[16,512]{1,0:T(8,128)(2,1)S(1)}, bf16[3,16,2,128]{3,2,1,0:T(2,128)(2,1)S(1)}, bf16[3,16,512]{2,1,0:T(8,128)(2,1)S(1)}, pred[]{:...) while((s32[]{:T(128)}, bf16[16,512]{1,0:T(8,128)(2,1)S(1)}, ...), condition=%wide.region_6.7_spmd, body=%wide.region_0.6_spmd.sunk | while | flops 312584256 | bytes 28671032 | solution.py:191
  7.4 23.8 %all_gather.16 = bf16[16,8192]{1,0:T(8,128)(2,1)S(1)} all-gather(bf16[16,512]{1,0:T(8,128)(2,1)S(1)} %bitcast_select_fusion.3), channel_id=1, replica_groups=mesh['segment'=2,'tensor'=16] {'tensor'}, dimensions={1}, use_global_device_ids=true | all-gather | bytes 278528 | tf_op jit(solution)/shard_map/while/body/eval_jaxpr/all_gather | solution.py:100
  33.5 4.6 %fusion.85 = f32[16,512]{1,0:T(8,128)S(1)} fusion(bf16[8192,512]{1,0:T(8,128)(2,1)} %get-tuple-element.675, bf16[16,8192]{1,0:T(8,128)(2,1)S(1)} %all_gather.16, f32[8192]{0:T(1024)S(1)} %bitcast.173, f32[16]{0:T(128)S(1)} %add_rsqrt_fusion.2), kind=kOutput, calls=%fused_computation.40.clone.1 | convolution fusion | flops 134742016 | bytes 8716352 | tf_op jit(solution)/shard_map/while/body/eval_jaxpr/dot_general | solution.py:102
  39.3 2.0 gather_fusion.1
  41.4 1.7 fusion.88
  43.5 3.5 %collective-permute-done.1 = bf16[16,2,128]{2,0,1:T(8,128)(2,1)S(1)} collective-permute-done((bf16[16,2,128]{2,0,1:T(8,128)(2,1)S(1)}, bf16[16,2,128]{2,0,1:T(8,128)(2,1)S(1)}, u32[]{:S(2)}, u32[]{:S(2)}) %collective-permute-start.1) | collective-permute-done | bytes 8224 | tf_op jit(solution)/shard_map/while/body/eval_jaxpr/ppermute | solution.py:111
  47.2 3.6 %collective-permute-done.2 = bf16[16,2,256]{2,0,1:T(8,128)(2,1)S(1)} collective-permute-done((bf16[16,2,256]{2,0,1:T(8,128)(2,1)S(1)}, bf16[16,2,256]{2,0,1:T(8,128)(2,1)S(1)}, u32[]{:S(2)}, u32[]{:S(2)}) %collective-permute-start.2) | collective-permute-done | bytes 16416 | tf_op jit(solution)/shard_map/while/body/eval_jaxpr/ppermute | solution.py:111
  51.1 4.6 %collective-permute-done.3 = bf16[16,2,512]{2,0,1:T(8,128)(2,1)S(1)} collective-permute-done((bf16[16,2,512]{2,0,1:T(8,128)(2,1)S(1)}, bf16[16,2,512]{2,0,1:T(8,128)(2,1)S(1)}, u32[]{:S(2)}, u32[]{:S(2)}) %collective-permute-start.3) | collective-permute-done | bytes 32800 | tf_op jit(solution)/shard_map/while/body/eval_jaxpr/ppermute | solution.py:111
  58.1 1.5 fusion.96
  59.9 17.8 %all_gather.17 = bf16[16,8192]{1,0:T(8,128)(2,1)S(1)} all-gather(bf16[16,512]{1,0:T(8,128)(2,1)S(1)} %bitcast.178), channel_id=1, replica_groups=mesh['segment'=2,'tensor'=16] {'tensor'}, dimensions={1}, use_global_device_ids=true | all-gather | bytes 278528 | tf_op jit(solution)/shard_map/while/body/eval_jaxpr/all_gather | solution.py:166
  77.7 4.6 %fusion.98 = bf16[16,512]{1,0:T(8,128)(2,1)S(1)} fusion(bf16[16,8192]{1,0:T(8,128)(2,1)S(1)} %all_gather.17, bf16[8192,512]{1,0:T(8,128)(2,1)} %get-tuple-element.681, bf16[16,512]{1,0:T(8,128)(2,1)S(1)} %bitcast_select_fusion.3), kind=kOutput, calls=%fused_computation.17.clone.1 | convolution fusion | flops 134242304 | bytes 8683520 | tf_op jit(solution)/shard_map/while/body/eval_jaxpr/dot_general | solution.py:86
  82.3 1.5 collective-permute-start.4
  84.5 1.6 collective-permute-done.4
  88.1 19.9 %all_gather.16 = bf16[16,8192]{1,0:T(8,128)(2,1)S(1)} all-gather(bf16[16,512]{1,0:T(8,128)(2,1)S(1)} %bitcast_select_fusion.3), channel_id=1, replica_groups=mesh['segment'=2,'tensor'=16] {'tensor'}, dimensions={1}, use_global_device_ids=true | all-gather | bytes 278528 | tf_op jit(solution)/shard_map/while/body/eval_jaxpr/all_gather | solution.py:100
  110.3 4.6 %fusion.85 = f32[16,512]{1,0:T(8,128)S(1)} fusion(bf16[8192,512]{1,0:T(8,128)(2,1)} %get-tuple-element.675, bf16[16,8192]{1,0:T(8,128)(2,1)S(1)} %all_gather.16, f32[8192]{0:T(1024)S(1)} %bitcast.173, f32[16]{0:T(128)S(1)} %add_rsqrt_fusion.2), kind=kOutput, calls=%fused_computation.40.clone.1 | convolution fusion | flops 134742016 | bytes 8716352 | tf_op jit(solution)/shard_map/while/body/eval_jaxpr/dot_general | solution.py:102
  116.1 2.0 gather_fusion.1
  118.2 1.7 fusion.88
  120.3 3.5 %collective-permute-done.1 = bf16[16,2,128]{2,0,1:T(8,128)(2,1)S(1)} collective-permute-done((bf16[16,2,128]{2,0,1:T(8,128)(2,1)S(1)}, bf16[16,2,128]{2,0,1:T(8,128)(2,1)S(1)}, u32[]{:S(2)}, u32[]{:S(2)}) %collective-permute-start.1) | collective-permute-done | bytes 8224 | tf_op jit(solution)/shard_map/while/body/eval_jaxpr/ppermute | solution.py:111
  124.0 3.6 %collective-permute-done.2 = bf16[16,2,256]{2,0,1:T(8,128)(2,1)S(1)} collective-permute-done((bf16[16,2,256]{2,0,1:T(8,128)(2,1)S(1)}, bf16[16,2,256]{2,0,1:T(8,128)(2,1)S(1)}, u32[]{:S(2)}, u32[]{:S(2)}) %collective-permute-start.2) | collective-permute-done | bytes 16416 | tf_op jit(solution)/shard_map/while/body/eval_jaxpr/ppermute | solution.py:111
  127.9 4.6 %collective-permute-done.3 = bf16[16,2,512]{2,0,1:T(8,128)(2,1)S(1)} collective-permute-done((bf16[16,2,512]{2,0,1:T(8,128)(2,1)S(1)}, bf16[16,2,512]{2,0,1:T(8,128)(2,1)S(1)}, u32[]{:S(2)}, u32[]{:S(2)}) %collective-permute-start.3) | collective-permute-done | bytes 32800 | tf_op jit(solution)/shard_map/while/body/eval_jaxpr/ppermute | solution.py:111
  134.9 1.5 fusion.96
  136.7 17.8 %all_gather.17 = bf16[16,8192]{1,0:T(8,128)(2,1)S(1)} all-gather(bf16[16,512]{1,0:T(8,128)(2,1)S(1)} %bitcast.178), channel_id=1, replica_groups=mesh['segment'=2,'tensor'=16] {'tensor'}, dimensions={1}, use_global_device_ids=true | all-gather | bytes 278528 | tf_op jit(solution)/shard_map/while/body/eval_jaxpr/all_gather | solution.py:166
  154.5 4.6 %fusion.98 = bf16[16,512]{1,0:T(8,128)(2,1)S(1)} fusion(bf16[16,8192]{1,0:T(8,128)(2,1)S(1)} %all_gather.17, bf16[8192,512]{1,0:T(8,128)(2,1)} %get-tuple-element.681, bf16[16,512]{1,0:T(8,128)(2,1)S(1)} %bitcast_select_fusion.3), kind=kOutput, calls=%fused_computation.17.clone.1 | convolution fusion | flops 134242304 | bytes 8683520 | tf_op jit(solution)/shard_map/while/body/eval_jaxpr/dot_general | solution.py:86
  159.1 1.5 collective-permute-start.4
  161.3 1.6 collective-permute-done.4
  164.9 19.9 %all_gather.16 = bf16[16,8192]{1,0:T(8,128)(2,1)S(1)} all-gather(bf16[16,512]{1,0:T(8,128)(2,1)S(1)} %bitcast_select_fusion.3), channel_id=1, replica_groups=mesh['segment'=2,'tensor'=16] {'tensor'}, dimensions={1}, use_global_device_ids=true | all-gather | bytes 278528 | tf_op jit(solution)/shard_map/while/body/eval_jaxpr/all_gather | solution.py:100
  187.1 4.6 %fusion.85 = f32[16,512]{1,0:T(8,128)S(1)} fusion(bf16[8192,512]{1,0:T(8,128)(2,1)} %get-tuple-element.675, bf16[16,8192]{1,0:T(8,128)(2,1)S(1)} %all_gather.16, f32[8192]{0:T(1024)S(1)} %bitcast.173, f32[16]{0:T(128)S(1)} %add_rsqrt_fusion.2), kind=kOutput, calls=%fused_computation.40.clone.1 | convolution fusion | flops 134742016 | bytes 8716352 | tf_op jit(solution)/shard_map/while/body/eval_jaxpr/dot_general | solution.py:102
  192.9 2.0 gather_fusion.1
  195.0 1.7 fusion.88
  197.1 3.5 %collective-permute-done.1 = bf16[16,2,128]{2,0,1:T(8,128)(2,1)S(1)} collective-permute-done((bf16[16,2,128]{2,0,1:T(8,128)(2,1)S(1)}, bf16[16,2,128]{2,0,1:T(8,128)(2,1)S(1)}, u32[]{:S(2)}, u32[]{:S(2)}) %collective-permute-start.1) | collective-permute-done | bytes 8224 | tf_op jit(solution)/shard_map/while/body/eval_jaxpr/ppermute | solution.py:111
  200.8 3.6 %collective-permute-done.2 = bf16[16,2,256]{2,0,1:T(8,128)(2,1)S(1)} collective-permute-done((bf16[16,2,256]{2,0,1:T(8,128)(2,1)S(1)}, bf16[16,2,256]{2,0,1:T(8,128)(2,1)S(1)}, u32[]{:S(2)}, u32[]{:S(2)}) %collective-permute-start.2) | collective-permute-done | bytes 16416 | tf_op jit(solution)/shard_map/while/body/eval_jaxpr/ppermute | solution.py:111
  204.7 4.6 %collective-permute-done.3 = bf16[16,2,512]{2,0,1:T(8,128)(2,1)S(1)} collective-permute-done((bf16[16,2,512]{2,0,1:T(8,128)(2,1)S(1)}, bf16[16,2,512]{2,0,1:T(8,128)(2,1)S(1)}, u32[]{:S(2)}, u32[]{:S(2)}) %collective-permute-start.3) | collective-permute-done | bytes 32800 | tf_op jit(solution)/shard_map/while/body/eval_jaxpr/ppermute | solution.py:111
  211.7 1.5 fusion.96
  213.5 17.8 %all_gather.17 = bf16[16,8192]{1,0:T(8,128)(2,1)S(1)} all-gather(bf16[16,512]{1,0:T(8,128)(2,1)S(1)} %bitcast.178), channel_id=1, replica_groups=mesh['segment'=2,'tensor'=16] {'tensor'}, dimensions={1}, use_global_device_ids=true | all-gather | bytes 278528 | tf_op jit(solution)/shard_map/while/body/eval_jaxpr/all_gather | solution.py:166
  231.3 4.6 %fusion.98 = bf16[16,512]{1,0:T(8,128)(2,1)S(1)} fusion(bf16[16,8192]{1,0:T(8,128)(2,1)S(1)} %all_gather.17, bf16[8192,512]{1,0:T(8,128)(2,1)} %get-tuple-element.681, bf16[16,512]{1,0:T(8,128)(2,1)S(1)} %bitcast_select_fusion.3), kind=kOutput, calls=%fused_computation.17.clone.1 | convolution fusion | flops 134242304 | bytes 8683520 | tf_op jit(solution)/shard_map/while/body/eval_jaxpr/dot_general | solution.py:86
  235.9 1.5 collective-permute-start.4
  238.1 1.6 collective-permute-done.4
  241.7 19.9 %all_gather.16 = bf16[16,8192]{1,0:T(8,128)(2,1)S(1)} all-gather(bf16[16,512]{1,0:T(8,128)(2,1)S(1)} %bitcast_select_fusion.3), channel_id=1, replica_groups=mesh['segment'=2,'tensor'=16] {'tensor'}, dimensions={1}, use_global_device_ids=true | all-gather | bytes 278528 | tf_op jit(solution)/shard_map/while/body/eval_jaxpr/all_gather | solution.py:100
  263.9 4.6 %fusion.85 = f32[16,512]{1,0:T(8,128)S(1)} fusion(bf16[8192,512]{1,0:T(8,128)(2,1)} %get-tuple-element.675, bf16[16,8192]{1,0:T(8,128)(2,1)S(1)} %all_gather.16, f32[8192]{0:T(1024)S(1)} %bitcast.173, f32[16]{0:T(128)S(1)} %add_rsqrt_fusion.2), kind=kOutput, calls=%fused_computation.40.clone.1 | convolution fusion | flops 134742016 | bytes 8716352 | tf_op jit(solution)/shard_map/while/body/eval_jaxpr/dot_general | solution.py:102
  269.7 2.0 gather_fusion.1
  271.8 1.7 fusion.88
  273.9 3.5 %collective-permute-done.1 = bf16[16,2,128]{2,0,1:T(8,128)(2,1)S(1)} collective-permute-done((bf16[16,2,128]{2,0,1:T(8,128)(2,1)S(1)}, bf16[16,2,128]{2,0,1:T(8,128)(2,1)S(1)}, u32[]{:S(2)}, u32[]{:S(2)}) %collective-permute-start.1) | collective-permute-done | bytes 8224 | tf_op jit(solution)/shard_map/while/body/eval_jaxpr/ppermute | solution.py:111
  277.6 3.6 %collective-permute-done.2 = bf16[16,2,256]{2,0,1:T(8,128)(2,1)S(1)} collective-permute-done((bf16[16,2,256]{2,0,1:T(8,128)(2,1)S(1)}, bf16[16,2,256]{2,0,1:T(8,128)(2,1)S(1)}, u32[]{:S(2)}, u32[]{:S(2)}) %collective-permute-start.2) | collective-permute-done | bytes 16416 | tf_op jit(solution)/shard_map/while/body/eval_jaxpr/ppermute | solution.py:111
  281.5 4.6 %collective-permute-done.3 = bf16[16,2,512]{2,0,1:T(8,128)(2,1)S(1)} collective-permute-done((bf16[16,2,512]{2,0,1:T(8,128)(2,1)S(1)}, bf16[16,2,512]{2,0,1:T(8,128)(2,1)S(1)}, u32[]{:S(2)}, u32[]{:S(2)}) %collective-permute-start.3) | collective-permute-done | bytes 32800 | tf_op jit(solution)/shard_map/while/body/eval_jaxpr/ppermute | solution.py:111
  288.5 1.5 fusion.96
  290.3 17.8 %all_gather.17 = bf16[16,8192]{1,0:T(8,128)(2,1)S(1)} all-gather(bf16[16,512]{1,0:T(8,128)(2,1)S(1)} %bitcast.178), channel_id=1, replica_groups=mesh['segment'=2,'tensor'=16] {'tensor'}, dimensions={1}, use_global_device_ids=true | all-gather | bytes 278528 | tf_op jit(solution)/shard_map/while/body/eval_jaxpr/all_gather | solution.py:166
  308.1 4.6 %fusion.98 = bf16[16,512]{1,0:T(8,128)(2,1)S(1)} fusion(bf16[16,8192]{1,0:T(8,128)(2,1)S(1)} %all_gather.17, bf16[8192,512]{1,0:T(8,128)(2,1)} %get-tuple-element.681, bf16[16,512]{1,0:T(8,128)(2,1)S(1)} %bitcast_select_fusion.3), kind=kOutput, calls=%fused_computation.17.clone.1 | convolution fusion | flops 134242304 | bytes 8683520 | tf_op jit(solution)/shard_map/while/body/eval_jaxpr/dot_general | solution.py:86
  314.9 1.6 collective-permute-done.4
  (285 shorter events, 40.6 us)
Async XLA Ops:
  0.0 5.2 %copy-start.5 = (s32[16,2]{0,1:T(2,128)S(1)}, s32[16,2]{0,1:T(2,128)}, u32[]{:S(2)}) copy-start(s32[16,2]{0,1:T(2,128)} %param.17) | copy-start | bytes 388
  0.0 5.3 %copy-start.1 = (bf16[1,1,3,128,256]{4,3,2,1,0:T(8,128)(2,1)S(1)}, bf16[1,1,3,128,256]{4,3,2,1,0:T(8,128)(2,1)}, u32[]{:S(2)}) copy-start(bf16[1,1,3,128,256]{4,3,2,1,0:T(8,128)(2,1)} %param.16) | copy-start | bytes 589828
  0.0 5.3 %copy-start.2 = (bf16[1,8192,2,64]{1,3,2,0:T(8,128)(2,1)S(1)}, bf16[1,8192,2,64]{1,3,2,0:T(8,128)(2,1)}, u32[]{:S(2)}) copy-start(bf16[1,8192,2,64]{1,3,2,0:T(8,128)(2,1)} %param.14) | copy-start | bytes 6291460
  0.0 5.3 %copy-start.3 = (f32[1,8192]{1,0:T(1,128)S(1)}, f32[1,8192]{1,0:T(1,128)}, u32[]{:S(2)}) copy-start(f32[1,8192]{1,0:T(1,128)} %param.12) | copy-start | bytes 98308
  0.0 5.3 %copy-start = (s32[16]{0:T(128)S(1)}, s32[16]{0:T(128)}, u32[]{:S(2)}) copy-start(s32[16]{0:T(128)} %param.18) | copy-start | bytes 196
  32.3 11.0 %collective-permute-start = (bf16[16,2,64]{2,0,1:T(8,128)(2,1)S(1)}, bf16[16,2,64]{2,0,1:T(8,128)(2,1)S(1)}, u32[]{:S(2)}, u32[]{:S(2)}) collective-permute-start(bf16[16,2,64]{2,0,1:T(8,128)(2,1)S(1)} %convolution_convert_fusion.2), channel_id=1, source_target_pairs={{0,1},{1,0},{2,3},{3,2},{4,5},{5,4},{6,7},{7,6},{8,9},{9,8},{10,11... | collective-permute-start | bytes 12296 | tf_op jit(solution)/shard_map/while/body/eval_jaxpr/ppermute | solution.py:111
  43.4 3.7 %collective-permute-start.1 = (bf16[16,2,128]{2,0,1:T(8,128)(2,1)S(1)}, bf16[16,2,128]{2,0,1:T(8,128)(2,1)S(1)}, u32[]{:S(2)}, u32[]{:S(2)}) collective-permute-start(bf16[16,2,128]{2,0,1:T(8,128)(2,1)S(1)} %maximum_select_fusion.12), channel_id=1, source_target_pairs={{0,2},{1,3},{2,0},{3,1},{4,6},{5,7},{6,4},{7,5},{8,10},{9,11},{10,... | collective-permute-start | bytes 24584 | tf_op jit(solution)/shard_map/while/body/eval_jaxpr/ppermute | solution.py:111
  47.1 3.7 %collective-permute-start.2 = (bf16[16,2,256]{2,0,1:T(8,128)(2,1)S(1)}, bf16[16,2,256]{2,0,1:T(8,128)(2,1)S(1)}, u32[]{:S(2)}, u32[]{:S(2)}) collective-permute-start(bf16[16,2,256]{2,0,1:T(8,128)(2,1)S(1)} %maximum_select_fusion.13), channel_id=1, source_target_pairs={{0,4},{1,5},{2,6},{3,7},{4,0},{5,1},{6,2},{7,3},{8,12},{9,13},{10,... | collective-permute-start | bytes 49160 | tf_op jit(solution)/shard_map/while/body/eval_jaxpr/ppermute | solution.py:111
  50.8 4.9 %collective-permute-start.3 = (bf16[16,2,512]{2,0,1:T(8,128)(2,1)S(1)}, bf16[16,2,512]{2,0,1:T(8,128)(2,1)S(1)}, u32[]{:S(2)}, u32[]{:S(2)}) collective-permute-start(bf16[16,2,512]{2,0,1:T(8,128)(2,1)S(1)} %maximum_select_fusion.14), channel_id=1, source_target_pairs={{0,8},{1,9},{2,10},{3,11},{4,12},{5,13},{6,14},{7,15},{8,0},{9,1},... | collective-permute-start | bytes 98312 | tf_op jit(solution)/shard_map/while/body/eval_jaxpr/ppermute | solution.py:111
  82.3 3.8 %collective-permute-start.4 = (bf16[16,512]{1,0:T(8,128)(2,1)S(1)}, bf16[16,512]{1,0:T(8,128)(2,1)S(1)}, u32[]{:S(2)}, u32[]{:S(2)}) collective-permute-start(bf16[16,512]{1,0:T(8,128)(2,1)S(1)} %fusion.98), channel_id=1, source_target_pairs={{16,0},{0,16},{17,1},{1,17},{18,2},{2,18},{19,3},{3,19},{20,4},{4,... | collective-permute-start | bytes 49160 | tf_op jit(solution)/shard_map/while/body/eval_jaxpr/ppermute | solution.py:21
  109.1 11.0 %collective-permute-start = (bf16[16,2,64]{2,0,1:T(8,128)(2,1)S(1)}, bf16[16,2,64]{2,0,1:T(8,128)(2,1)S(1)}, u32[]{:S(2)}, u32[]{:S(2)}) collective-permute-start(bf16[16,2,64]{2,0,1:T(8,128)(2,1)S(1)} %convolution_convert_fusion.2), channel_id=1, source_target_pairs={{0,1},{1,0},{2,3},{3,2},{4,5},{5,4},{6,7},{7,6},{8,9},{9,8},{10,11... | collective-permute-start | bytes 12296 | tf_op jit(solution)/shard_map/while/body/eval_jaxpr/ppermute | solution.py:111
  120.2 3.7 %collective-permute-start.1 = (bf16[16,2,128]{2,0,1:T(8,128)(2,1)S(1)}, bf16[16,2,128]{2,0,1:T(8,128)(2,1)S(1)}, u32[]{:S(2)}, u32[]{:S(2)}) collective-permute-start(bf16[16,2,128]{2,0,1:T(8,128)(2,1)S(1)} %maximum_select_fusion.12), channel_id=1, source_target_pairs={{0,2},{1,3},{2,0},{3,1},{4,6},{5,7},{6,4},{7,5},{8,10},{9,11},{10,... | collective-permute-start | bytes 24584 | tf_op jit(solution)/shard_map/while/body/eval_jaxpr/ppermute | solution.py:111
  123.9 3.7 %collective-permute-start.2 = (bf16[16,2,256]{2,0,1:T(8,128)(2,1)S(1)}, bf16[16,2,256]{2,0,1:T(8,128)(2,1)S(1)}, u32[]{:S(2)}, u32[]{:S(2)}) collective-permute-start(bf16[16,2,256]{2,0,1:T(8,128)(2,1)S(1)} %maximum_select_fusion.13), channel_id=1, source_target_pairs={{0,4},{1,5},{2,6},{3,7},{4,0},{5,1},{6,2},{7,3},{8,12},{9,13},{10,... | collective-permute-start | bytes 49160 | tf_op jit(solution)/shard_map/while/body/eval_jaxpr/ppermute | solution.py:111
  127.6 4.9 %collective-permute-start.3 = (bf16[16,2,512]{2,0,1:T(8,128)(2,1)S(1)}, bf16[16,2,512]{2,0,1:T(8,128)(2,1)S(1)}, u32[]{:S(2)}, u32[]{:S(2)}) collective-permute-start(bf16[16,2,512]{2,0,1:T(8,128)(2,1)S(1)} %maximum_select_fusion.14), channel_id=1, source_target_pairs={{0,8},{1,9},{2,10},{3,11},{4,12},{5,13},{6,14},{7,15},{8,0},{9,1},... | collective-permute-start | bytes 98312 | tf_op jit(solution)/shard_map/while/body/eval_jaxpr/ppermute | solution.py:111
  159.1 3.8 %collective-permute-start.4 = (bf16[16,512]{1,0:T(8,128)(2,1)S(1)}, bf16[16,512]{1,0:T(8,128)(2,1)S(1)}, u32[]{:S(2)}, u32[]{:S(2)}) collective-permute-start(bf16[16,512]{1,0:T(8,128)(2,1)S(1)} %fusion.98), channel_id=1, source_target_pairs={{16,0},{0,16},{17,1},{1,17},{18,2},{2,18},{19,3},{3,19},{20,4},{4,... | collective-permute-start | bytes 49160 | tf_op jit(solution)/shard_map/while/body/eval_jaxpr/ppermute | solution.py:21
  185.9 11.0 %collective-permute-start = (bf16[16,2,64]{2,0,1:T(8,128)(2,1)S(1)}, bf16[16,2,64]{2,0,1:T(8,128)(2,1)S(1)}, u32[]{:S(2)}, u32[]{:S(2)}) collective-permute-start(bf16[16,2,64]{2,0,1:T(8,128)(2,1)S(1)} %convolution_convert_fusion.2), channel_id=1, source_target_pairs={{0,1},{1,0},{2,3},{3,2},{4,5},{5,4},{6,7},{7,6},{8,9},{9,8},{10,11... | collective-permute-start | bytes 12296 | tf_op jit(solution)/shard_map/while/body/eval_jaxpr/ppermute | solution.py:111
  197.0 3.7 %collective-permute-start.1 = (bf16[16,2,128]{2,0,1:T(8,128)(2,1)S(1)}, bf16[16,2,128]{2,0,1:T(8,128)(2,1)S(1)}, u32[]{:S(2)}, u32[]{:S(2)}) collective-permute-start(bf16[16,2,128]{2,0,1:T(8,128)(2,1)S(1)} %maximum_select_fusion.12), channel_id=1, source_target_pairs={{0,2},{1,3},{2,0},{3,1},{4,6},{5,7},{6,4},{7,5},{8,10},{9,11},{10,... | collective-permute-start | bytes 24584 | tf_op jit(solution)/shard_map/while/body/eval_jaxpr/ppermute | solution.py:111
  200.7 3.7 %collective-permute-start.2 = (bf16[16,2,256]{2,0,1:T(8,128)(2,1)S(1)}, bf16[16,2,256]{2,0,1:T(8,128)(2,1)S(1)}, u32[]{:S(2)}, u32[]{:S(2)}) collective-permute-start(bf16[16,2,256]{2,0,1:T(8,128)(2,1)S(1)} %maximum_select_fusion.13), channel_id=1, source_target_pairs={{0,4},{1,5},{2,6},{3,7},{4,0},{5,1},{6,2},{7,3},{8,12},{9,13},{10,... | collective-permute-start | bytes 49160 | tf_op jit(solution)/shard_map/while/body/eval_jaxpr/ppermute | solution.py:111
  204.4 4.9 %collective-permute-start.3 = (bf16[16,2,512]{2,0,1:T(8,128)(2,1)S(1)}, bf16[16,2,512]{2,0,1:T(8,128)(2,1)S(1)}, u32[]{:S(2)}, u32[]{:S(2)}) collective-permute-start(bf16[16,2,512]{2,0,1:T(8,128)(2,1)S(1)} %maximum_select_fusion.14), channel_id=1, source_target_pairs={{0,8},{1,9},{2,10},{3,11},{4,12},{5,13},{6,14},{7,15},{8,0},{9,1},... | collective-permute-start | bytes 98312 | tf_op jit(solution)/shard_map/while/body/eval_jaxpr/ppermute | solution.py:111
  235.9 3.8 %collective-permute-start.4 = (bf16[16,512]{1,0:T(8,128)(2,1)S(1)}, bf16[16,512]{1,0:T(8,128)(2,1)S(1)}, u32[]{:S(2)}, u32[]{:S(2)}) collective-permute-start(bf16[16,512]{1,0:T(8,128)(2,1)S(1)} %fusion.98), channel_id=1, source_target_pairs={{16,0},{0,16},{17,1},{1,17},{18,2},{2,18},{19,3},{3,19},{20,4},{4,... | collective-permute-start | bytes 49160 | tf_op jit(solution)/shard_map/while/body/eval_jaxpr/ppermute | solution.py:21
  262.7 11.0 %collective-permute-start = (bf16[16,2,64]{2,0,1:T(8,128)(2,1)S(1)}, bf16[16,2,64]{2,0,1:T(8,128)(2,1)S(1)}, u32[]{:S(2)}, u32[]{:S(2)}) collective-permute-start(bf16[16,2,64]{2,0,1:T(8,128)(2,1)S(1)} %convolution_convert_fusion.2), channel_id=1, source_target_pairs={{0,1},{1,0},{2,3},{3,2},{4,5},{5,4},{6,7},{7,6},{8,9},{9,8},{10,11... | collective-permute-start | bytes 12296 | tf_op jit(solution)/shard_map/while/body/eval_jaxpr/ppermute | solution.py:111
  273.8 3.7 %collective-permute-start.1 = (bf16[16,2,128]{2,0,1:T(8,128)(2,1)S(1)}, bf16[16,2,128]{2,0,1:T(8,128)(2,1)S(1)}, u32[]{:S(2)}, u32[]{:S(2)}) collective-permute-start(bf16[16,2,128]{2,0,1:T(8,128)(2,1)S(1)} %maximum_select_fusion.12), channel_id=1, source_target_pairs={{0,2},{1,3},{2,0},{3,1},{4,6},{5,7},{6,4},{7,5},{8,10},{9,11},{10,... | collective-permute-start | bytes 24584 | tf_op jit(solution)/shard_map/while/body/eval_jaxpr/ppermute | solution.py:111
  277.4 3.7 %collective-permute-start.2 = (bf16[16,2,256]{2,0,1:T(8,128)(2,1)S(1)}, bf16[16,2,256]{2,0,1:T(8,128)(2,1)S(1)}, u32[]{:S(2)}, u32[]{:S(2)}) collective-permute-start(bf16[16,2,256]{2,0,1:T(8,128)(2,1)S(1)} %maximum_select_fusion.13), channel_id=1, source_target_pairs={{0,4},{1,5},{2,6},{3,7},{4,0},{5,1},{6,2},{7,3},{8,12},{9,13},{10,... | collective-permute-start | bytes 49160 | tf_op jit(solution)/shard_map/while/body/eval_jaxpr/ppermute | solution.py:111
  281.2 4.9 %collective-permute-start.3 = (bf16[16,2,512]{2,0,1:T(8,128)(2,1)S(1)}, bf16[16,2,512]{2,0,1:T(8,128)(2,1)S(1)}, u32[]{:S(2)}, u32[]{:S(2)}) collective-permute-start(bf16[16,2,512]{2,0,1:T(8,128)(2,1)S(1)} %maximum_select_fusion.14), channel_id=1, source_target_pairs={{0,8},{1,9},{2,10},{3,11},{4,12},{5,13},{6,14},{7,15},{8,0},{9,1},... | collective-permute-start | bytes 98312 | tf_op jit(solution)/shard_map/while/body/eval_jaxpr/ppermute | solution.py:111
  312.7 3.8 %collective-permute-start.4 = (bf16[16,512]{1,0:T(8,128)(2,1)S(1)}, bf16[16,512]{1,0:T(8,128)(2,1)S(1)}, u32[]{:S(2)}, u32[]{:S(2)}) collective-permute-start(bf16[16,512]{1,0:T(8,128)(2,1)S(1)} %fusion.98), channel_id=1, source_target_pairs={{16,0},{0,16},{17,1},{1,17},{18,2},{2,18},{19,3},{3,19},{20,4},{4,... | collective-permute-start | bytes 49160 | tf_op jit(solution)/shard_map/while/body/eval_jaxpr/ppermute | solution.py:21
  316.5 0.6 copy-start.4
